TPU v7x, 128 devices: a whole 4x4x4 slice. The times are simulated.
128 devices in a mesh: px: 8 (over z, x_lo), py: 16 (over x_hi, y, core).
Axes of the slice: x: 4 (x_hi: 2, x_lo: 2; x = x_hi * 2 + x_lo), y: 4, z: 4, core: 2. Of those that a mesh axis runs over, the one named last changes fastest.
Arguments:
- loads: float32 [3, 128, 1024, 128], P(None, 'px', 'py'), may hold values from -6 to 6
- targets: float32 [3, 128, 1024, 128], P(None, 'px', 'py'), may hold values from -6 to 6
- anchor: float32 [128, 1024], P('px', 'py'), may hold values from 0.05 to 0.5
- q_down: float32 [128, 1024], P('px', 'py'), may hold values from 0.5 to 2
- q_right: float32 [128, 1024], P('px', 'py'), may hold values from 0.5 to 2
- send_rows: int32 [8, 1024], P('px', 'py'), may hold values from 0 to 1023, as said below
- cable_a: int32 [8, 2048], P('px', 'py'), may hold values from 0 to 63, as said below
- cable_b: int32 [8, 2048], P('px', 'py'), may hold values from 0 to 63, as said below
- cable_count: int32 [8, 16], P('px', 'py'), may hold values from 1 to 128, 1024 in all within a row
- cable_q: float32 [8, 2048], P('px', 'py'), may hold values from 0.5 to 2
Outputs:
- shape_field: float32 [3, 128, 1024, 128], P(None, 'px', 'py')
- adjoint_field: float32 [3, 128, 1024, 128], P(None, 'px', 'py')
- grad_down: float32 [128, 1024], P('px', 'py')
- grad_right: float32 [128, 1024], P('px', 'py')
- grad_long: float32 [8, 2048], P('px', 'py')
Inputs may be any that keep to these rules, and one draw needn't show every extreme that they name: `send_rows`: within each block of 4 entries (one tile lending to one owner) the nodes differ. `cable_a`: codes of one cable's two ends differ. `cable_b`: codes of one cable's two ends differ. `cable_count`: each plan-x row's counts sum to 1024; some owner has all 128 slots live.
All inputs are finite; a program needn't handle non-finite values. No bound on the sum of `cable_count` on one device may be relied on, other than what follows from the above.
Results may differ from a plain program's by a relative error of at most 0.00011.
Values sent between devices are 32-bit elements; how exact they have to be, the bound alone decides.
A program may use at most 128 MiB of HBM per device.

v0:
```python
import functools

import jax
import jax.numpy as jnp
from jax import lax
from jax.experimental import pallas as pl
from jax.experimental.pallas import tpu as pltpu
from jax.sharding import PartitionSpec as P

MESH = pl.DeviceIdType.MESH
F32 = jnp.float32
BF16 = jnp.bfloat16
HIGHEST = lax.Precision.HIGHEST

STEPS = 7
ROUNDS = STEPS - 1
TX, TY, V = 16, 64, 128
NODES = TX * TY
SLOTS = 64
LOW, HIGH = 0.05, 2.0
THETA = (HIGH + LOW) / 2.0
DELTA = (HIGH - LOW) / 2.0


def coefficients():
    sigma = THETA / DELTA
    rho = 1.0 / sigma
    pairs = []
    for _ in range(ROUNDS):
        rho_new = 1.0 / (2.0 * sigma - rho)
        pairs.append((rho_new * rho, 2.0 * rho_new / DELTA))
        rho = rho_new
    return pairs


COEF = coefficients()


def coef_of(round_):
    a, b = (jnp.float32(value) for value in COEF[-1])
    for k in range(ROUNDS - 1):
        a = jnp.where(round_ == k, jnp.float32(COEF[k][0]), a)
        b = jnp.where(round_ == k, jnp.float32(COEF[k][1]), b)
    return a, b


def split2(x):
    high = x.astype(BF16)
    return high, (x - high.astype(F32)).astype(BF16)


def split3(x):
    high = x.astype(BF16)
    rest = x - high.astype(F32)
    mid = rest.astype(BF16)
    return high, mid, (rest - mid.astype(F32)).astype(BF16)


def dot(a, b):
    return jnp.dot(a, b, preferred_element_type=F32)


def dot_t(a, b, precision=None):
    return lax.dot_general(
        a, b, (((1,), (1,)), ((), ())), precision=precision, preferred_element_type=F32
    )


def iota(shape, dim):
    return lax.broadcasted_iota(jnp.int32, shape, dim)


(
    S_P1, R_P1, S_P2, R_P2, S_UP, R_UP, S_DN, R_DN, S_LF, R_LF, S_RT, R_RT,
    S_CAB, R_CAB, S_DQ, R_DQ, S_QD, R_QD, S_QR, R_QR, S_SH, R_SH,
    S_GD, R_GD, S_GR, R_GR, S_HD, R_HD, S_HR, R_HR, L_B, L_T, L_S, L_A,
) = range(0, 68, 2)
N_SEM = 68


def kernel(
    n_px, n_py,
    loads, targets, anchor, q_down, q_right, rows_s, rows_v, cab_a, cab_b, count, cab_q,
    shape_out, adjoint_out, down_out, right_out, long_out,
    R, D, X, S, T, SF, GD, WD, WR, WL, INV, ONE, F3, C3, LH, LL, LM,
    rg_l, d_l, x_l, t_l, inv_l, Y, XS, recv1, recvS, Fs, frecv,
    up, dn, lf, rt, cl, cr, cab_s, cab_r, dq_s, dq_r, qd_s, qd_r, qr_s, qr_r,
    gdS, grS, gdA, grA, c0S, c0A, stS, PD, PR, sem,
):
    px = lax.axis_index("px")
    py = lax.axis_index("py")
    half = n_py // 2
    h0 = py // half
    q0 = py % half
    px_next, px_prev = (px + 1) % n_px, (px + n_px - 1) % n_px
    py_next, py_prev = (py + 1) % n_py, (py + n_py - 1) % n_py

    def remote(src, dst, s, r, to):
        return pltpu.make_async_remote_copy(
            src, dst, sem.at[s], sem.at[r], device_id=to, device_id_type=MESH
        )

    def wait_bytes(view, s):
        pltpu.make_async_copy(view, view, sem.at[s]).wait()

    load_b = pltpu.make_async_copy(loads, R, sem.at[L_B])
    load_t = pltpu.make_async_copy(targets, T, sem.at[L_T])
    load_b.start()
    load_t.start()

    barrier = pltpu.get_barrier_semaphore()
    for i in range(1, n_py):
        pl.semaphore_signal(barrier, inc=1, device_id=(px, (py + i) % n_py), device_id_type=MESH)
    pl.semaphore_signal(barrier, inc=1, device_id=(px_next, py), device_id_type=MESH)
    pl.semaphore_signal(barrier, inc=1, device_id=(px_prev, py), device_id_type=MESH)

    live = iota((1, 128), 1) < count[0, 0]
    q_live = jnp.where(live, cab_q[...], 0.0)
    row8 = iota((8, 128), 0)
    cab_s[...] = jnp.where(
        row8 == 0,
        cab_a[...].astype(F32),
        jnp.where(row8 == 1, cab_b[...].astype(F32), jnp.where(row8 == 2, q_live, 0.0)),
    )
    m_id = iota((128, 128), 0)
    code = (m_id // 8 * 4 + m_id % 4).astype(F32)
    m_half = m_id % 8 // 4

    def ends(values, which):
        mine = m_half == which
        at_a = jnp.where(mine & (code == values[0:1]), 1.0, 0.0)
        at_b = jnp.where(mine & (code == values[1:2]), 1.0, 0.0)
        return at_a, at_b

    at_a, at_b = ends(cab_s[...], h0)
    slot_q = jnp.sum((at_a + at_b) * q_live, axis=1, keepdims=True)
    dq_s[...] = jnp.broadcast_to(slot_q, (128, 128)).reshape(n_py, 8, 128)
    qd_s[...] = jnp.concatenate(
        [jnp.broadcast_to(q_down[TX - 1 : TX, :], (8, TY)), jnp.zeros((8, 128 - TY), F32)], axis=1
    )
    qr_s[...] = jnp.concatenate([q_right[...], jnp.zeros((TX, 128 - TY), F32)], axis=1)

    pl.semaphore_wait(barrier, n_py + 1)

    for i in range(1, n_py):
        t = (py + i) % n_py
        remote(dq_s.at[t], dq_r.at[py], S_DQ, R_DQ, (px, t)).start()
    cab_copy = remote(cab_s, cab_r, S_CAB, R_CAB, (px, (py + half) % n_py))
    qd_copy = remote(qd_s, qd_r, S_QD, R_QD, (px_next, py))
    qr_copy = remote(qr_s, qr_r, S_QR, R_QR, (px, py_next))
    cab_copy.start()
    qd_copy.start()
    qr_copy.start()
    dq_r[py] = dq_s[py]

    p_id, l_id = iota((SLOTS, 3 * SLOTS), 0), iota((SLOTS, 3 * SLOTS), 1) % SLOTS
    perm = jnp.where(p_id == (l_id // 8 + half * (l_id % 8 // 4)) * 4 + l_id % 4, 1.0, 0.0)
    row_f = jnp.broadcast_to(rows_v[...].astype(F32), (8, SLOTS))
    in_lanes = jnp.dot(row_f, perm, precision=HIGHEST, preferred_element_type=F32)[0:1]
    in_rows = lax.dot_general(
        perm[:, :SLOTS], row_f, (((0,), (1,)), ((), ())), precision=HIGHEST, preferred_element_type=F32
    )[:, 0:1]
    C3[...] = jnp.where(
        jnp.broadcast_to(in_rows, (SLOTS, 3 * SLOTS)) == in_lanes, 1.0, 0.0
    ).astype(BF16)

    def one_hot(i, carry):
        node = (iota((TY, 3 * SLOTS), 0) + i * TY).astype(F32)
        ONE[pl.ds(pl.multiple_of(i * TY, TY), TY)] = jnp.where(node == in_lanes, 1.0, 0.0).astype(BF16)
        return carry

    lax.fori_loop(0, TX, one_hot, 0)

    qd_copy.wait()
    qr_copy.wait()
    gi = iota((TX, TY), 0) + px * TX
    gj = iota((TX, TY), 1) + py * TY
    w_down = jnp.where(gi < n_px * TX - 1, q_down[...], 0.0)
    w_right = jnp.where(gj < n_py * TY - 1, q_right[...], 0.0)
    prev_down = jnp.where(px > 0, qd_r[0:1, :TY], 0.0)
    prev_right = jnp.where(py > 0, qr_r[:, TY - 1 : TY], 0.0)
    w_up = jnp.concatenate([prev_down, w_down[:-1]], 0)
    w_left = jnp.concatenate([prev_right, w_right[:, :-1]], 1)
    diag = anchor[...] + w_down + w_up + w_right + w_left
    stacked = jnp.concatenate(
        [diag, w_down, w_right, w_left, jnp.broadcast_to(prev_down, (8, TY))], 0
    )
    eye = jnp.where(iota((TY, TY), 0) == iota((TY, TY), 1), 1.0, 0.0)
    columns = dot_t(eye, stacked, HIGHEST)

    def spread(col):
        return jnp.broadcast_to(columns[:, col : col + 1], (TY, V))

    WD[0:TY] = spread(4 * TX)
    for i in range(TX):
        at = pl.ds(i * TY, TY)
        GD[at] = spread(i)
        WD[pl.ds((i + 1) * TY, TY)] = spread(TX + i)
        WR[at] = spread(2 * TX + i)
        WL[at] = spread(3 * TX + i)

    cab_copy.wait()
    pa, pb = ends(cab_r[...], 1 - h0)
    inc_own, inc_other = at_a - at_b, pa - pb
    LM[...] = dot_t(inc_own * q_live, inc_own, HIGHEST) + dot_t(
        inc_other * cab_r[2:3], inc_other, HIGHEST
    )
    mine_rows = LM[pl.ds(pl.multiple_of(h0 * SLOTS, SLOTS), SLOTS)]
    l_high, l_low = split2(mine_rows)
    LH[:, 0:128] = l_high
    LH[:, 128:256] = l_high
    LL[...] = l_low

    wait_bytes(dq_r.at[pl.ds(0, n_py - 1)], R_DQ)
    slot_sum = (dq_r[0:half] + dq_r[half:]).reshape(SLOTS, V)
    LD = dot(ONE[...], jnp.concatenate(split3(slot_sum), 0))
    INV[...] = 1.0 / (GD[...] + LD)
    wait_bytes(dq_s.at[pl.ds(0, n_py - 1)], S_DQ)

    def gather(src, dst):
        def rows_of(w, carry):
            for e in range(8):
                node = rows_s[0, (w + half * (e // 4)) * 4 + e % 4]
                for c in range(3):
                    dst[c, pl.ds(w * 8 + e, 1), :] = src[c, pl.ds(node, 1), :]
            return carry

        lax.fori_loop(0, half, rows_of, 0)

    def gather_inv(w, carry):
        for e in range(8):
            node = rows_s[0, (w + half * (e // 4)) * 4 + e % 4]
            inv_l[pl.ds(w * 8 + e, 1), :] = INV[pl.ds(node, 1), :]
        return carry

    lax.fori_loop(0, half, gather_inv, 0)

    def send_lent(src, dst, s, r):
        for i in range(1, n_py):
            t = (py + i) % n_py
            remote(src.at[t % half], dst.at[py], s, r, (px, t)).start()
        dst[py] = src[q0]

    def put(dst, c, value):
        dst[:, c] = value.reshape(half, 8, V)

    load_b.wait()
    gather(R, rg_l)
    for c in range(3):
        first = inv_l[...] * rg_l[c] * (1.0 / THETA)
        d_l[c] = first
        x_l[c] = first
        put(Y, c, first)
    send_lent(Y, recv1.at[0], S_P1, R_P1)
    load_t.wait()
    gather(T, t_l)

    last = 2 * ROUNDS
    save_shape = pltpu.make_async_copy(S, shape_out, sem.at[L_S])
    shape_down = remote(S.at[:, pl.ds(0, TY)], gdS, S_GD, R_GD, (px_prev, py))
    shape_right = remote(c0S, grS, S_GR, R_GR, (px, py_prev))

    def spans(i):
        return pl.ds(pl.multiple_of(i * TY, TY), TY)

    def scatter(lo, hi):
        SF[lo * TY : hi * TY] = dot(ONE[lo * TY : hi * TY], F3[...])

    def advance(i, a, b):
        at = spans(i)
        inv = INV[at] * b
        for c in range(3):
            r = R[c, at] - SF[at, c * V : (c + 1) * V]
            R[c, at] = r
            d = a * D[c, at] + inv * r
            D[c, at] = d
            X[c, at] = X[c, at] + d

    def begin(i):
        at = spans(i)
        inv = INV[at] * (1.0 / THETA)
        for c in range(3):
            d = inv * R[c, at]
            D[c, at] = d
            X[c, at] = d

    def turn(i, a, b):
        at = spans(i)
        inv = INV[at]
        for c in range(3):
            r = R[c, at] - SF[at, c * V : (c + 1) * V]
            x = X[c, at] + (a * D[c, at] + (inv * b) * r)
            S[c, at] = x
            r = x - T[c, at]
            R[c, at] = r
            d = inv * r * (1.0 / THETA)
            D[c, at] = d
            X[c, at] = d

    def each(fn, lo, hi):
        def body(i, carry):
            fn(i)
            return carry

        lax.fori_loop(lo, hi, body, 0)

    def stencil(i, par, above, below):
        at = spans(i)
        gd, wu, wd, wr, wl = GD[at], WD[at], WD[spans(i + 1)], WR[at], WL[at]
        row = iota((TY, V), 0)
        for c in range(3):
            d = D[c, at]
            left = jnp.where(row == 0, lf[par, c, pl.ds(i, 1), :], pltpu.roll(d, 1, 0))
            right = jnp.where(row == TY - 1, rt[par, c, pl.ds(i, 1), :], pltpu.roll(d, TY - 1, 0))
            near = wu * above(c) + wd * below(c) + wl * left + wr * right
            R[c, at] = R[c, at] - (gd * d - near)

    def round_(t, carry):
        par = t % 2
        first, middle = t == 0, t == ROUNDS
        usual = jnp.logical_and(t != 0, t != ROUNDS)
        a_prev, b_prev = coef_of((t + ROUNDS - 1) % ROUNDS)
        a_next, b_next = coef_of(t % ROUNDS)

        @pl.when(t != 0)
        def _():
            scatter(0, 1)
            scatter(TX - 1, TX)

        @pl.when(first)
        def _():
            begin(0)
            begin(TX - 1)

        @pl.when(usual)
        def _():
            advance(0, a_prev, b_prev)
            advance(TX - 1, a_prev, b_prev)

        @pl.when(middle)
        def _():
            turn(0, a_prev, b_prev)
            turn(TX - 1, a_prev, b_prev)

        to_next = remote(
            D.at[:, pl.ds((TX - 1) * TY, TY)], up.at[par], S_UP, R_UP + par, (px_next, py)
        )
        to_prev = remote(D.at[:, pl.ds(0, TY)], dn.at[par], S_DN, R_DN + par, (px_prev, py))
        to_next.start()
        to_prev.start()

        @pl.when(t != 0)
        def _():
            scatter(1, TX - 1)

        @pl.when(first)
        def _():
            each(begin, 1, TX - 1)

        @pl.when(usual)
        def _():
            each(lambda i: advance(i, a_prev, b_prev), 1, TX - 1)

        @pl.when(middle)
        def _():
            each(lambda i: turn(i, a_prev, b_prev), 1, TX - 1)

        for c in range(3):
            for i in range(TX):
                cl[c, i : i + 1] = D[c, i * TY : i * TY + 1]
                cr[c, i : i + 1] = D[c, (i + 1) * TY - 1 : (i + 1) * TY]
        to_right = remote(cr, lf.at[par], S_LF, R_LF + par, (px, py_next))
        to_left = remote(cl, rt.at[par], S_RT, R_RT + par, (px, py_prev))
        to_right.start()
        to_left.start()

        @pl.when(middle)
        def _():
            for c in range(3):
                for i in range(TX):
                    c0S[c, i : i + 1] = S[c, i * TY : i * TY + 1]
            save_shape.start()
            shape_down.start()
            shape_right.start()

        wait_bytes(recv1.at[0, pl.ds(0, n_py - 1)], R_P1 + par)
        for c in range(3):
            high, low = split2(recv1[par, :, c].reshape(128, V))
            force = dot(LH[...], jnp.concatenate([high, low], 0)) + dot(LL[...], high)
            put(Fs, c, force)
        for i in range(1, half):
            q = (q0 + i) % half
            remote(Fs.at[q], frecv.at[q0], S_P2, R_P2, (px, h0 * half + q)).start()
        frecv[q0] = Fs[q0]

        to_right.wait()
        to_left.wait()
        each(
            lambda i: stencil(
                i, par, lambda c: D[c, spans(i - 1)], lambda c: D[c, spans(i + 1)]
            ),
            1,
            TX - 1,
        )
        to_next.wait()
        to_prev.wait()
        stencil(0, par, lambda c: up[par, c], lambda c: D[c, spans(1)])
        stencil(TX - 1, par, lambda c: D[c, spans(TX - 2)], lambda c: dn[par, c])
        gather(R, rg_l)
        wait_bytes(recv1.at[0, pl.ds(0, n_py - 1)], S_P1)

        wait_bytes(frecv.at[pl.ds(0, half - 1)], R_P2)
        for c in range(3):
            high, mid, low = split3(frecv[:, c].reshape(SLOTS, V))
            lanes = pl.ds(c * V, V)
            F3[0:SLOTS, lanes] = high
            F3[SLOTS : 2 * SLOTS, lanes] = mid
            F3[2 * SLOTS :, lanes] = low
        at_node = dot(C3[...], F3[...])
        for c in range(3):
            r = rg_l[c] - at_node[:, c * V : (c + 1) * V]
            d = a_next * d_l[c] + (b_next * inv_l[...]) * r
            d_l[c] = d
            x_l[c] = x_l[c] + d
            put(Y, c, d)

        @pl.when(t == ROUNDS - 1)
        def _():
            for c in range(3):
                put(XS, c, x_l[c])
                d = inv_l[...] * (x_l[c] - t_l[c]) * (1.0 / THETA)
                d_l[c] = d
                x_l[c] = d
                put(Y, c, d)

        @pl.when(t == last - 1)
        def _():
            for c in range(3):
                put(Y, c, x_l[c])

        send_lent(Y, recv1.at[1 - par], S_P1, R_P1 + 1 - par)

        @pl.when(t == ROUNDS - 1)
        def _():
            send_lent(XS, recvS, S_SH, R_SH)

        wait_bytes(frecv.at[pl.ds(0, half - 1)], S_P2)
        return carry

    lax.fori_loop(0, last, round_, 0)

    a, b = COEF[-1]
    scatter(0, TX)
    each(lambda i: advance(i, a, b), 0, TX)
    for c in range(3):
        for i in range(TX):
            c0A[c, i : i + 1] = X[c, i * TY : i * TY + 1]
    adjoint_down = remote(X.at[:, pl.ds(0, TY)], gdA, S_HD, R_HD, (px_prev, py))
    adjoint_right = remote(c0A, grA, S_HR, R_HR, (px, py_prev))
    adjoint_down.start()
    adjoint_right.start()
    save_adjoint = pltpu.make_async_copy(X, adjoint_out, sem.at[L_A])
    save_adjoint.start()


    def stretches(view, store):
        at_a_, at_b_ = ends(cab_s[...], h0)
        inc_ = (at_a_ - at_b_).astype(BF16)
        total = None
        for c in range(3):
            out = None
            for part in split3(view[:, c].reshape(128, V)):
                piece = lax.dot_general(
                    inc_, part, (((0,), (0,)), ((), ())), preferred_element_type=F32
                )
                out = piece if out is None else out + piece
            if store:
                stS[c] = out
            else:
                term = out * stS[c]
                total = term if total is None else total + term
        return total

    def lane_sums(values):
        ones = jnp.ones((8, V), BF16)
        out = None
        for part in split3(values):
            piece = dot_t(ones, part)
            out = piece if out is None else out + piece
        return out[0:1] * (-1.0 / V)

    wait_bytes(recvS.at[pl.ds(0, n_py - 1)], R_SH)
    wait_bytes(recvS.at[pl.ds(0, n_py - 1)], S_SH)
    stretches(recvS, True)
    shape_down.wait()
    shape_right.wait()

    def down(i, below_s, below_a):
        at = spans(i)
        total = None
        for c in range(3):
            term = (X[c, at] - below_a(c)) * (S[c, at] - below_s(c))
            total = term if total is None else total + term
        PD[at] = total

    each(
        lambda i: down(i, lambda c: S[c, spans(i + 1)], lambda c: X[c, spans(i + 1)]), 0, TX - 1
    )
    adjoint_right.wait()

    def beside(i):
        at = spans(i)
        row = iota((TY, V), 0)
        total = None
        for c in range(3):
            s, x = S[c, at], X[c, at]
            s_next = jnp.where(row == TY - 1, grS[c, pl.ds(i, 1), :], pltpu.roll(s, TY - 1, 0))
            x_next = jnp.where(row == TY - 1, grA[c, pl.ds(i, 1), :], pltpu.roll(x, TY - 1, 0))
            term = (x - x_next) * (s - s_next)
            total = term if total is None else total + term
        PR[at] = total

    each(beside, 0, TX)
    right_sums = lane_sums(PR[...])
    adjoint_down.wait()
    down(TX - 1, lambda c: gdS[c], lambda c: gdA[c])
    down_sums = lane_sums(PD[...])
    for i in range(TX):
        lanes = slice(i * TY, (i + 1) * TY)
        down_out[i : i + 1] = down_sums[:, lanes]
        right_out[i : i + 1] = right_sums[:, lanes]
    down_out[...] = jnp.where(gi < n_px * TX - 1, down_out[...], 0.0)
    right_out[...] = jnp.where(gj < n_py * TY - 1, right_out[...], 0.0)

    par = last % 2
    wait_bytes(recv1.at[0, pl.ds(0, n_py - 1)], R_P1 + par)
    long_sums = lane_sums(stretches(recv1.at[par], False))
    long_out[...] = jnp.where(live, long_sums, 0.0)
    wait_bytes(recv1.at[0, pl.ds(0, n_py - 1)], S_P1)
    save_shape.wait()
    save_adjoint.wait()


def per_device(
    n_px, n_py,
    loads, targets, anchor, q_down, q_right, send_rows, cable_a, cable_b, cable_count, cable_q,
):
    half = n_py // 2
    field = (3, NODES, V)
    vmem = pl.BlockSpec(memory_space=pltpu.VMEM)
    smem = pl.BlockSpec(memory_space=pltpu.SMEM)
    anywhere = pl.BlockSpec(memory_space=pl.ANY)

    def scratch(*shape, dtype=F32):
        return pltpu.VMEM(shape, dtype)

    lent = (half, 3, 8, V)
    shape_field, adjoint_field, grad_down, grad_right, grad_long = pl.pallas_call(
        functools.partial(kernel, n_px, n_py),
        out_shape=(
            jax.ShapeDtypeStruct(field, F32),
            jax.ShapeDtypeStruct(field, F32),
            jax.ShapeDtypeStruct((TX, TY), F32),
            jax.ShapeDtypeStruct((TX, TY), F32),
            jax.ShapeDtypeStruct((1, 128), F32),
        ),
        in_specs=[anywhere, anywhere, vmem, vmem, vmem, smem, vmem, vmem, vmem, smem, vmem],
        out_specs=(anywhere, anywhere, vmem, vmem, vmem),
        scratch_shapes=[
            scratch(*field),
            scratch(*field),
            scratch(*field),
            scratch(*field),
            scratch(*field),
            scratch(NODES, 3 * V),
            scratch(NODES, V),
            scratch(NODES + TY, V),
            scratch(NODES, V),
            scratch(NODES, V),
            scratch(NODES, V),
            scratch(NODES, 3 * SLOTS, dtype=BF16),
            scratch(3 * SLOTS, 3 * V, dtype=BF16),
            scratch(SLOTS, 3 * SLOTS, dtype=BF16),
            scratch(SLOTS, 256, dtype=BF16),
            scratch(SLOTS, 128, dtype=BF16),
            scratch(128, 128),
            scratch(3, SLOTS, V),
            scratch(3, SLOTS, V),
            scratch(3, SLOTS, V),
            scratch(3, SLOTS, V),
            scratch(SLOTS, V),
            scratch(*lent),
            scratch(*lent),
            scratch(2, n_py, 3, 8, V),
            scratch(n_py, 3, 8, V),
            scratch(*lent),
            scratch(*lent),
            scratch(2, 3, TY, V),
            scratch(2, 3, TY, V),
            scratch(2, 3, TX, V),
            scratch(2, 3, TX, V),
            scratch(3, TX, V),
            scratch(3, TX, V),
            scratch(8, 128),
            scratch(8, 128),
            scratch(n_py, 8, 128),
            scratch(n_py, 8, 128),
            scratch(8, 128),
            scratch(8, 128),
            scratch(TX, 128),
            scratch(TX, 128),
            scratch(3, TY, V),
            scratch(3, TX, V),
            scratch(3, TY, V),
            scratch(3, TX, V),
            scratch(3, TX, V),
            scratch(3, TX, V),
            scratch(3, 128, V),
            scratch(NODES, V),
            scratch(NODES, V),
            pltpu.SemaphoreType.DMA((N_SEM,)),
        ],
        compiler_params=pltpu.CompilerParams(
            collective_id=0, has_side_effects=True, vmem_limit_bytes=40 << 20
        ),
        name="cable_net",
    )(
        loads.reshape(field),
        targets.reshape(field),
        anchor,
        q_down,
        q_right,
        send_rows,
        send_rows,
        cable_a,
        cable_b,
        cable_count,
        cable_q,
    )
    tile = (3, TX, TY, V)
    return shape_field.reshape(tile), adjoint_field.reshape(tile), grad_down, grad_right, grad_long


def solution(mesh):
    field = P(None, "px", "py", None)
    flat = P("px", "py")
    return jax.shard_map(
        functools.partial(per_device, mesh.shape["px"], mesh.shape["py"]),
        mesh=mesh,
        in_specs=(field, field) + (flat,) * 8,
        out_specs=(field, field, flat, flat, flat),
        check_vma=False,
    )
```

profile of v0, /device:TPU:25, one launch (start us, length us, event | category | flops | bytes accessed | tf_op | source)
XLA Modules:
  0.0 166.2 jit_solution(15012526573602887304)
XLA Ops:
  1.3 0.0 copy-start
  1.3 1.4 copy-done
  2.7 0.0 copy-start.1
  2.7 1.4 copy-done.1
  4.1 0.0 copy-start.2
  4.1 0.7 copy-done.2
  4.8 0.0 copy-start.3
  4.8 0.7 copy-done.3
  5.5 0.0 copy-start.4
  5.5 0.7 copy-done.4
  6.2 0.0 copy-start.5
  6.2 0.7 copy-done.5
  6.8 0.0 copy-start.6
  6.8 0.7 copy-done.6
  7.5 0.0 copy-start.7
  7.5 0.7 copy-done.7
  8.2 0.0 copy-start.8
  8.2 0.7 copy-done.8
  8.8 153.4 %cable_net.1 = (f32[3,1024,128]{2,1,0:T(8,128)S(1)}, f32[3,1024,128]{2,1,0:T(8,128)S(1)}, f32[16,64]{1,0:T(8,128)S(1)}, f32[16,64]{1,0:T(8,128)S(1)}, f32[1,128]{1,0:T(1,128)S(1)}) custom-call(f32[3,1024,128]{2,1,0:T(8,128)S(1)} %bitcast.4, f32[3,1024,128]{2,1,0:T(8,128)S(1)} %bitcast.5, f32[16,64]{1,0:T(8,128)S(1)} %copy-done.2, f32[16,64]{1,0:T(8,128)S(1)} %copy-done.3, ...), custom_call_target="tpu_custom_call" | custom-call | tf_op jit(solution)/shard_map/cable_net/pallas_call | solution.py:558
  162.2 1.1 copy.21
  163.3 1.1 copy.22
  164.5 0.6 copy.23
  165.1 0.6 copy.24
  165.7 0.5 copy.25
Async XLA Ops:
  1.3 1.4 copy-start
  2.7 1.4 copy-start.1
  4.1 0.7 copy-start.2
  4.8 0.7 copy-start.3
  5.5 0.7 copy-start.4
  6.2 0.7 copy-start.5
  6.8 0.7 copy-start.6
  7.5 0.7 copy-start.7
  8.2 0.7 copy-start.8
where the time goes:
time: 167 us; the launch traced here: 166 us
  Pallas kernels  153 us (92%)
  local copies, waits for them, and re-layouts  11.5 us (7%)
    pallas_call x1, Pallas kernels, per_device(): pl.pallas_call(functools.partial(kernel, n_px, n_py), out_shape=(jax.Shap...  153 us
    unnamed x23, local copies, waits for them, and re-layouts  11.5 us

commit v1 on v0

--- a/solution.py
+++ b/solution.py
@@ -18,6 +18,7 @@
 NODES = TX * TY
 SLOTS = 64
 LOW, HIGH = 0.05, 2.0
+LIMIT = 60 << 20
 THETA = (HIGH + LOW) / 2.0
 DELTA = (HIGH - LOW) / 2.0
 
@@ -72,20 +73,22 @@
 
 (
     S_P1, R_P1, S_P2, R_P2, S_UP, R_UP, S_DN, R_DN, S_LF, R_LF, S_RT, R_RT,
-    S_CAB, R_CAB, S_DQ, R_DQ, S_QD, R_QD, S_QR, R_QR, S_SH, R_SH,
+    S_CAB, R_CAB, S_DQ, R_DQ, S_QD, R_QD, S_QR, R_QR, S_SH, R_SH, S_AD, R_AD,
     S_GD, R_GD, S_GR, R_GR, S_HD, R_HD, S_HR, R_HR, L_B, L_T, L_S, L_A,
-) = range(0, 68, 2)
-N_SEM = 68
+    L_0, L_1, L_2, L_3, L_4, L_5, L_6, L_7,
+) = range(0, 88, 2)
+N_SEM = 88
 
 
 def kernel(
     n_px, n_py,
-    loads, targets, anchor, q_down, q_right, rows_s, rows_v, cab_a, cab_b, count, cab_q,
+    loads, targets, anchor_h, q_down_h, q_right_h, rows_s, rows_h, cab_a_h, cab_b_h, count, cab_q_h,
     shape_out, adjoint_out, down_out, right_out, long_out,
-    R, D, X, S, T, SF, GD, WD, WR, WL, INV, ONE, F3, C3, LH, LL, LM,
-    rg_l, d_l, x_l, t_l, inv_l, Y, XS, recv1, recvS, Fs, frecv,
+    R, D, X, S, T, SF, GD, WD, WR, WL, INV, ONE, F2, CR, L3, IO, IP,
+    rg_l, d_l, x_l, t_l, inv_l, Y, XS, recv1, recvS, recvA, Fs, frecv,
     up, dn, lf, rt, cl, cr, cab_s, cab_r, dq_s, dq_r, qd_s, qd_r, qr_s, qr_r,
-    gdS, grS, gdA, grA, c0S, c0A, stS, PD, PR, sem,
+    gdS, grS, gdA, grA, c0S, c0A, stS, PD, PR,
+    anchor, q_down, q_right, rows_v, cab_a, cab_b, cab_q, sem,
 ):
     px = lax.axis_index("px")
     py = lax.axis_index("py")
@@ -105,6 +108,16 @@
 
     load_b = pltpu.make_async_copy(loads, R, sem.at[L_B])
     load_t = pltpu.make_async_copy(targets, T, sem.at[L_T])
+    small = [
+        pltpu.make_async_copy(src, dst, sem.at[s])
+        for src, dst, s in (
+            (cab_a_h, cab_a, L_0), (cab_b_h, cab_b, L_1),
+            (cab_q_h, cab_q, L_3), (q_down_h, q_down, L_4), (q_right_h, q_right, L_5),
+            (rows_h, rows_v, L_6), (anchor_h, anchor, L_7),
+        )
+    ]
+    for copy in small:
+        copy.start()
     load_b.start()
     load_t.start()
 
@@ -113,6 +126,22 @@
         pl.semaphore_signal(barrier, inc=1, device_id=(px, (py + i) % n_py), device_id_type=MESH)
     pl.semaphore_signal(barrier, inc=1, device_id=(px_next, py), device_id_type=MESH)
     pl.semaphore_signal(barrier, inc=1, device_id=(px_prev, py), device_id_type=MESH)
+
+    wide = half // 2
+    y0, c0 = q0 // 2, q0 % 2
+    order = sorted(
+        (v for v in ((dx, dy, dc) for dx in (0, 1) for dy in range(wide) for dc in (0, 1)) if any(v)),
+        key=lambda v: -(2 * v[0] + min(v[1], wide - v[1])),
+    )
+
+    def other(dx, dy, dc):
+        return (h0 + dx) % 2, (y0 + dy) % wide * 2 + (c0 + dc) % 2
+
+    peers = [other(*v) for v in order]
+    near_peers = [other(*v) for v in order if v[0] == 0]
+
+    for copy in small:
+        copy.wait()
 
     live = iota((1, 128), 1) < count[0, 0]
     q_live = jnp.where(live, cab_q[...], 0.0)
@@ -140,10 +169,30 @@
     )
     qr_s[...] = jnp.concatenate([q_right[...], jnp.zeros((TX, 128 - TY), F32)], axis=1)
 
+    p_id, l_id = iota((SLOTS, 2 * SLOTS), 0), iota((SLOTS, 2 * SLOTS), 1) % SLOTS
+    perm = jnp.where(p_id == (l_id // 8 + half * (l_id % 8 // 4)) * 4 + l_id % 4, 1.0, 0.0)
+    row_f = jnp.broadcast_to(rows_v[...].astype(F32), (8, SLOTS))
+    in_lanes = jnp.dot(row_f, perm, precision=HIGHEST, preferred_element_type=F32)[0:1]
+    in_rows = lax.dot_general(
+        perm[:, :SLOTS], row_f, (((0,), (1,)), ((), ())), precision=HIGHEST, preferred_element_type=F32
+    )[:, 0:1]
+    CR[0:SLOTS] = jnp.where(
+        jnp.broadcast_to(in_rows, (SLOTS, 2 * SLOTS)) == in_lanes, 1.0, 0.0
+    ).astype(BF16)
+
+    def one_hot(i, carry):
+        node = (iota((TY, 2 * SLOTS), 0) + i * TY).astype(F32)
+        ONE[pl.ds(pl.multiple_of(i * TY, TY), TY)] = jnp.where(node == in_lanes, 1.0, 0.0).astype(BF16)
+        return carry
+
+    lax.fori_loop(0, TX, one_hot, 0)
+    CR[SLOTS : SLOTS + TY] = ONE[0:TY]
+    CR[SLOTS + TY :] = ONE[NODES - TY :]
+
     pl.semaphore_wait(barrier, n_py + 1)
 
-    for i in range(1, n_py):
-        t = (py + i) % n_py
+    for h, q in peers:
+        t = h * half + q
         remote(dq_s.at[t], dq_r.at[py], S_DQ, R_DQ, (px, t)).start()
     cab_copy = remote(cab_s, cab_r, S_CAB, R_CAB, (px, (py + half) % n_py))
     qd_copy = remote(qd_s, qd_r, S_QD, R_QD, (px_next, py))
@@ -152,24 +201,6 @@
     qd_copy.start()
     qr_copy.start()
     dq_r[py] = dq_s[py]
-
-    p_id, l_id = iota((SLOTS, 3 * SLOTS), 0), iota((SLOTS, 3 * SLOTS), 1) % SLOTS
-    perm = jnp.where(p_id == (l_id // 8 + half * (l_id % 8 // 4)) * 4 + l_id % 4, 1.0, 0.0)
-    row_f = jnp.broadcast_to(rows_v[...].astype(F32), (8, SLOTS))
-    in_lanes = jnp.dot(row_f, perm, precision=HIGHEST, preferred_element_type=F32)[0:1]
-    in_rows = lax.dot_general(
-        perm[:, :SLOTS], row_f, (((0,), (1,)), ((), ())), precision=HIGHEST, preferred_element_type=F32
-    )[:, 0:1]
-    C3[...] = jnp.where(
-        jnp.broadcast_to(in_rows, (SLOTS, 3 * SLOTS)) == in_lanes, 1.0, 0.0
-    ).astype(BF16)
-
-    def one_hot(i, carry):
-        node = (iota((TY, 3 * SLOTS), 0) + i * TY).astype(F32)
-        ONE[pl.ds(pl.multiple_of(i * TY, TY), TY)] = jnp.where(node == in_lanes, 1.0, 0.0).astype(BF16)
-        return carry
-
-    lax.fori_loop(0, TX, one_hot, 0)
 
     qd_copy.wait()
     qr_copy.wait()
@@ -202,20 +233,13 @@
     cab_copy.wait()
     pa, pb = ends(cab_r[...], 1 - h0)
     inc_own, inc_other = at_a - at_b, pa - pb
-    LM[...] = dot_t(inc_own * q_live, inc_own, HIGHEST) + dot_t(
-        inc_other * cab_r[2:3], inc_other, HIGHEST
-    )
-    mine_rows = LM[pl.ds(pl.multiple_of(h0 * SLOTS, SLOTS), SLOTS)]
-    l_high, l_low = split2(mine_rows)
-    LH[:, 0:128] = l_high
-    LH[:, 128:256] = l_high
-    LL[...] = l_low
-
-    wait_bytes(dq_r.at[pl.ds(0, n_py - 1)], R_DQ)
-    slot_sum = (dq_r[0:half] + dq_r[half:]).reshape(SLOTS, V)
-    LD = dot(ONE[...], jnp.concatenate(split3(slot_sum), 0))
-    INV[...] = 1.0 / (GD[...] + LD)
-    wait_bytes(dq_s.at[pl.ds(0, n_py - 1)], S_DQ)
+    IO[...] = inc_own
+    IP[...] = inc_other
+    of_half = pl.ds(pl.multiple_of(h0 * SLOTS, SLOTS), SLOTS)
+    matrix = dot_t(inc_own * q_live, IO[of_half], HIGHEST) + dot_t(
+        inc_other * cab_r[2:3], IP[of_half], HIGHEST
+    )
+    L3[...] = jnp.concatenate([matrix, matrix - matrix.astype(BF16).astype(F32)], 1).astype(BF16)
 
     def gather(src, dst):
         def rows_of(w, carry):
@@ -227,33 +251,40 @@
 
         lax.fori_loop(0, half, rows_of, 0)
 
-    def gather_inv(w, carry):
+    def gather_diag(w, carry):
         for e in range(8):
             node = rows_s[0, (w + half * (e // 4)) * 4 + e % 4]
-            inv_l[pl.ds(w * 8 + e, 1), :] = INV[pl.ds(node, 1), :]
+            inv_l[pl.ds(w * 8 + e, 1), :] = GD[pl.ds(node, 1), :]
         return carry
 
-    lax.fori_loop(0, half, gather_inv, 0)
-
-    def send_lent(src, dst, s, r):
-        for i in range(1, n_py):
-            t = (py + i) % n_py
-            remote(src.at[t % half], dst.at[py], s, r, (px, t)).start()
+    def send_all(src, dst, s, r):
+        for h, q in peers:
+            remote(src.at[q], dst.at[py], s, r, (px, h * half + q)).start()
         dst[py] = src[q0]
 
+    def send_lent():
+        for h, q in near_peers:
+            remote(Y.at[q], recv1.at[q0], S_P1, R_P1, (px, h * half + q)).start()
+        recv1[q0] = Y[q0]
+
     def put(dst, c, value):
-        dst[:, c] = value.reshape(half, 8, V)
-
+        dst[:, c] = value.reshape(dst.shape[0], 8, V)
+
+    lax.fori_loop(0, half, gather_diag, 0)
     load_b.wait()
     gather(R, rg_l)
+
+    wait_bytes(dq_r.at[pl.ds(0, n_py - 1)], R_DQ)
+    slot_sum = (dq_r[0:half] + dq_r[half:]).reshape(SLOTS, V)
+    slot_sum = jnp.concatenate(split2(slot_sum), 0)
+    inv_l[...] = 1.0 / (inv_l[...] + dot(CR[0:SLOTS], slot_sum))
     for c in range(3):
         first = inv_l[...] * rg_l[c] * (1.0 / THETA)
         d_l[c] = first
         x_l[c] = first
         put(Y, c, first)
-    send_lent(Y, recv1.at[0], S_P1, R_P1)
-    load_t.wait()
-    gather(T, t_l)
+    send_lent()
+    INV[...] = 1.0 / (GD[...] + dot(ONE[...], slot_sum))
 
     last = 2 * ROUNDS
     save_shape = pltpu.make_async_copy(S, shape_out, sem.at[L_S])
@@ -264,7 +295,7 @@
         return pl.ds(pl.multiple_of(i * TY, TY), TY)
 
     def scatter(lo, hi):
-        SF[lo * TY : hi * TY] = dot(ONE[lo * TY : hi * TY], F3[...])
+        SF[lo * TY : hi * TY] = dot(ONE[lo * TY : hi * TY], F2[...])
 
     def advance(i, a, b):
         at = spans(i)
@@ -315,17 +346,30 @@
             near = wu * above(c) + wd * below(c) + wl * left + wr * right
             R[c, at] = R[c, at] - (gd * d - near)
 
+    def stretches(view, store):
+        at_a_, at_b_ = ends(cab_s[...], h0)
+        inc_ = (at_a_ - at_b_).astype(BF16)
+        total = None
+        for c in range(3):
+            out = None
+            for part in split3(view[:, c].reshape(128, V)):
+                piece = lax.dot_general(
+                    inc_, part, (((0,), (0,)), ((), ())), preferred_element_type=F32
+                )
+                out = piece if out is None else out + piece
+            if store:
+                stS[c] = out
+            else:
+                term = out * stS[c]
+                total = term if total is None else total + term
+        return total
+
     def round_(t, carry):
         par = t % 2
         first, middle = t == 0, t == ROUNDS
         usual = jnp.logical_and(t != 0, t != ROUNDS)
         a_prev, b_prev = coef_of((t + ROUNDS - 1) % ROUNDS)
         a_next, b_next = coef_of(t % ROUNDS)
-
-        @pl.when(t != 0)
-        def _():
-            scatter(0, 1)
-            scatter(TX - 1, TX)
 
         @pl.when(first)
         def _():
@@ -383,15 +427,27 @@
             shape_down.start()
             shape_right.start()
 
-        wait_bytes(recv1.at[0, pl.ds(0, n_py - 1)], R_P1 + par)
-        for c in range(3):
-            high, low = split2(recv1[par, :, c].reshape(128, V))
-            force = dot(LH[...], jnp.concatenate([high, low], 0)) + dot(LL[...], high)
-            put(Fs, c, force)
-        for i in range(1, half):
-            q = (q0 + i) % half
-            remote(Fs.at[q], frecv.at[q0], S_P2, R_P2, (px, h0 * half + q)).start()
-        frecv[q0] = Fs[q0]
+        wait_bytes(recv1.at[pl.ds(0, half - 1)], R_P1)
+        for c in range(3):
+            high, low = split2(recv1[:, c].reshape(SLOTS, V))
+            matrix = L3[...]
+            put(Fs, c, dot(matrix, jnp.concatenate([high, high], 0)) + dot(matrix[:, :SLOTS], low))
+        for h, q in peers:
+            to = h * half + q
+            remote(Fs.at[to], frecv.at[par, py], S_P2, R_P2 + par, (px, to)).start()
+        frecv[par, py] = Fs[py]
+
+        @pl.when(t == 0)
+        def _():
+            wait_bytes(dq_s.at[pl.ds(0, n_py - 1)], S_DQ)
+            load_t.wait()
+            gather(T, t_l)
+
+        @pl.when(t == ROUNDS + 1)
+        def _():
+            wait_bytes(recvS.at[pl.ds(0, n_py - 1)], R_SH)
+            wait_bytes(recvS.at[pl.ds(0, n_py - 1)], S_SH)
+            stretches(recvS, True)
 
         to_right.wait()
         to_left.wait()
@@ -407,22 +463,23 @@
         stencil(0, par, lambda c: up[par, c], lambda c: D[c, spans(1)])
         stencil(TX - 1, par, lambda c: D[c, spans(TX - 2)], lambda c: dn[par, c])
         gather(R, rg_l)
-        wait_bytes(recv1.at[0, pl.ds(0, n_py - 1)], S_P1)
-
-        wait_bytes(frecv.at[pl.ds(0, half - 1)], R_P2)
-        for c in range(3):
-            high, mid, low = split3(frecv[:, c].reshape(SLOTS, V))
+        wait_bytes(recv1.at[pl.ds(0, half - 1)], S_P1)
+
+        wait_bytes(frecv.at[0, pl.ds(0, n_py - 1)], R_P2 + par)
+        for c in range(3):
+            high, low = split2((frecv[par, 0:half, c] + frecv[par, half:, c]).reshape(SLOTS, V))
             lanes = pl.ds(c * V, V)
-            F3[0:SLOTS, lanes] = high
-            F3[SLOTS : 2 * SLOTS, lanes] = mid
-            F3[2 * SLOTS :, lanes] = low
-        at_node = dot(C3[...], F3[...])
-        for c in range(3):
-            r = rg_l[c] - at_node[:, c * V : (c + 1) * V]
+            F2[0:SLOTS, lanes] = high
+            F2[SLOTS:, lanes] = low
+        at_node = dot(CR[...], F2[...])
+        for c in range(3):
+            r = rg_l[c] - at_node[:SLOTS, c * V : (c + 1) * V]
             d = a_next * d_l[c] + (b_next * inv_l[...]) * r
             d_l[c] = d
             x_l[c] = x_l[c] + d
             put(Y, c, d)
+        SF[0:TY] = at_node[SLOTS : SLOTS + TY]
+        SF[NODES - TY :] = at_node[SLOTS + TY :]
 
         @pl.when(t == ROUNDS - 1)
         def _():
@@ -433,53 +490,36 @@
                 x_l[c] = d
                 put(Y, c, d)
 
-        @pl.when(t == last - 1)
-        def _():
-            for c in range(3):
-                put(Y, c, x_l[c])
-
-        send_lent(Y, recv1.at[1 - par], S_P1, R_P1 + 1 - par)
+        @pl.when(t != last - 1)
+        def _():
+            send_lent()
 
         @pl.when(t == ROUNDS - 1)
         def _():
-            send_lent(XS, recvS, S_SH, R_SH)
-
-        wait_bytes(frecv.at[pl.ds(0, half - 1)], S_P2)
+            send_all(XS, recvS, S_SH, R_SH)
+
+        wait_bytes(frecv.at[0, pl.ds(0, n_py - 1)], S_P2)
         return carry
 
     lax.fori_loop(0, last, round_, 0)
 
+    for c in range(3):
+        put(Y, c, x_l[c])
+    send_all(Y, recvA, S_AD, R_AD)
     a, b = COEF[-1]
-    scatter(0, TX)
-    each(lambda i: advance(i, a, b), 0, TX)
+    advance(0, a, b)
+    adjoint_down = remote(X.at[:, pl.ds(0, TY)], gdA, S_HD, R_HD, (px_prev, py))
+    adjoint_down.start()
+    scatter(1, TX - 1)
+    each(lambda i: advance(i, a, b), 1, TX)
+    save_adjoint = pltpu.make_async_copy(X, adjoint_out, sem.at[L_A])
+    save_adjoint.start()
     for c in range(3):
         for i in range(TX):
             c0A[c, i : i + 1] = X[c, i * TY : i * TY + 1]
-    adjoint_down = remote(X.at[:, pl.ds(0, TY)], gdA, S_HD, R_HD, (px_prev, py))
     adjoint_right = remote(c0A, grA, S_HR, R_HR, (px, py_prev))
-    adjoint_down.start()
     adjoint_right.start()
-    save_adjoint = pltpu.make_async_copy(X, adjoint_out, sem.at[L_A])
-    save_adjoint.start()
-
-
-    def stretches(view, store):
-        at_a_, at_b_ = ends(cab_s[...], h0)
-        inc_ = (at_a_ - at_b_).astype(BF16)
-        total = None
-        for c in range(3):
-            out = None
-            for part in split3(view[:, c].reshape(128, V)):
-                piece = lax.dot_general(
-                    inc_, part, (((0,), (0,)), ((), ())), preferred_element_type=F32
-                )
-                out = piece if out is None else out + piece
-            if store:
-                stS[c] = out
-            else:
-                term = out * stS[c]
-                total = term if total is None else total + term
-        return total
+
 
     def lane_sums(values):
         ones = jnp.ones((8, V), BF16)
@@ -489,9 +529,6 @@
             out = piece if out is None else out + piece
         return out[0:1] * (-1.0 / V)
 
-    wait_bytes(recvS.at[pl.ds(0, n_py - 1)], R_SH)
-    wait_bytes(recvS.at[pl.ds(0, n_py - 1)], S_SH)
-    stretches(recvS, True)
     shape_down.wait()
     shape_right.wait()
 
@@ -532,13 +569,33 @@
     down_out[...] = jnp.where(gi < n_px * TX - 1, down_out[...], 0.0)
     right_out[...] = jnp.where(gj < n_py * TY - 1, right_out[...], 0.0)
 
-    par = last % 2
-    wait_bytes(recv1.at[0, pl.ds(0, n_py - 1)], R_P1 + par)
-    long_sums = lane_sums(stretches(recv1.at[par], False))
+    wait_bytes(recvA.at[pl.ds(0, n_py - 1)], R_AD)
+    long_sums = lane_sums(stretches(recvA, False))
     long_out[...] = jnp.where(live, long_sums, 0.0)
-    wait_bytes(recv1.at[0, pl.ds(0, n_py - 1)], S_P1)
+    wait_bytes(recvA.at[pl.ds(0, n_py - 1)], S_AD)
     save_shape.wait()
     save_adjoint.wait()
+
+
+def save_kernel(shape_in, adjoint_in, down_in, right_in, long_in, *refs):
+    outs, (shape_v, adjoint_v, down_v, right_v, long_v, sem) = refs[:5], refs[5:]
+    parts = 4
+    rows = NODES // parts
+    moves = []
+    for src, held, dst in ((shape_in, shape_v, outs[0]), (adjoint_in, adjoint_v, outs[1])):
+        for p in range(parts):
+            at = (slice(None), pl.ds(p * rows, rows))
+            moves.append((src.at[at], held.at[at], dst.at[at]))
+    moves += [(down_in, down_v, outs[2]), (right_in, right_v, outs[3]), (long_in, long_v, outs[4])]
+    fetch = [pltpu.make_async_copy(a, b, sem.at[0, k]) for k, (a, b, _) in enumerate(moves)]
+    store = [pltpu.make_async_copy(b, c, sem.at[1, k]) for k, (_, b, c) in enumerate(moves)]
+    for copy in fetch:
+        copy.start()
+    for k, copy in enumerate(fetch):
+        copy.wait()
+        store[k].start()
+    for copy in store:
+        copy.wait()
 
 
 def per_device(
@@ -555,7 +612,7 @@
         return pltpu.VMEM(shape, dtype)
 
     lent = (half, 3, 8, V)
-    shape_field, adjoint_field, grad_down, grad_right, grad_long = pl.pallas_call(
+    results = pl.pallas_call(
         functools.partial(kernel, n_px, n_py),
         out_shape=(
             jax.ShapeDtypeStruct(field, F32),
@@ -564,7 +621,7 @@
             jax.ShapeDtypeStruct((TX, TY), F32),
             jax.ShapeDtypeStruct((1, 128), F32),
         ),
-        in_specs=[anywhere, anywhere, vmem, vmem, vmem, smem, vmem, vmem, vmem, smem, vmem],
+        in_specs=[anywhere] * 5 + [smem] + [anywhere] * 3 + [smem, anywhere],
         out_specs=(anywhere, anywhere, vmem, vmem, vmem),
         scratch_shapes=[
             scratch(*field),
@@ -578,11 +635,11 @@
             scratch(NODES, V),
             scratch(NODES, V),
             scratch(NODES, V),
-            scratch(NODES, 3 * SLOTS, dtype=BF16),
-            scratch(3 * SLOTS, 3 * V, dtype=BF16),
-            scratch(SLOTS, 3 * SLOTS, dtype=BF16),
-            scratch(SLOTS, 256, dtype=BF16),
-            scratch(SLOTS, 128, dtype=BF16),
+            scratch(NODES, 2 * SLOTS, dtype=BF16),
+            scratch(2 * SLOTS, 3 * V, dtype=BF16),
+            scratch(SLOTS + 2 * TY, 2 * SLOTS, dtype=BF16),
+            scratch(128, 2 * SLOTS, dtype=BF16),
+            scratch(128, 128),
             scratch(128, 128),
             scratch(3, SLOTS, V),
             scratch(3, SLOTS, V),
@@ -591,10 +648,11 @@
             scratch(SLOTS, V),
             scratch(*lent),
             scratch(*lent),
+            scratch(*lent),
+            scratch(n_py, 3, 8, V),
+            scratch(n_py, 3, 8, V),
+            scratch(n_py, 3, 8, V),
             scratch(2, n_py, 3, 8, V),
-            scratch(n_py, 3, 8, V),
-            scratch(*lent),
-            scratch(*lent),
             scratch(2, 3, TY, V),
             scratch(2, 3, TY, V),
             scratch(2, 3, TX, V),
@@ -618,10 +676,17 @@
             scratch(3, 128, V),
             scratch(NODES, V),
             scratch(NODES, V),
+            scratch(TX, TY),
+            scratch(TX, TY),
+            scratch(TX, TY),
+            scratch(1, SLOTS, dtype=jnp.int32),
+            scratch(1, 128, dtype=jnp.int32),
+            scratch(1, 128, dtype=jnp.int32),
+            scratch(1, 128),
             pltpu.SemaphoreType.DMA((N_SEM,)),
         ],
         compiler_params=pltpu.CompilerParams(
-            collective_id=0, has_side_effects=True, vmem_limit_bytes=40 << 20
+            collective_id=0, has_side_effects=True, vmem_limit_bytes=LIMIT
         ),
         name="cable_net",
     )(
@@ -637,6 +702,16 @@
         cable_count,
         cable_q,
     )
+    shape_field, adjoint_field, grad_down, grad_right, grad_long = pl.pallas_call(
+        save_kernel,
+        out_shape=[jax.ShapeDtypeStruct(r.shape, F32) for r in results],
+        in_specs=[anywhere] * 5,
+        out_specs=[anywhere] * 5,
+        scratch_shapes=[pltpu.VMEM(r.shape, F32) for r in results]
+        + [pltpu.SemaphoreType.DMA((2, 11))],
+        compiler_params=pltpu.CompilerParams(vmem_limit_bytes=LIMIT),
+        name="save",
+    )(*results)
     tile = (3, TX, TY, V)
     return shape_field.reshape(tile), adjoint_field.reshape(tile), grad_down, grad_right, grad_long
 

time: 167 us -> 153 us (0.916)
  local copies, waits for them, and re-layouts: 11.5 us -> 0 us
  Pallas kernels: 153 us -> 151 us
    unnamed x23 -> x0, local copies, waits for them, and re-layouts: 11.5 us -> none
    pallas_call x1, Pallas kernels: 153 us -> 149 us  [per_device(): pl.pallas_call(functools.partial(kernel, n_px, n_py), out_shape=(jax.Shap...]
    pallas_call x0 -> x1, Pallas kernels: none -> 2.85 us  [per_device(): pl.pallas_call(save_kernel, out_shape=[jax.ShapeDtypeStruct(r.shape, F32)...]
where the time goes in v1:
time: 153 us
  Pallas kernels  151 us (99%)
    pallas_call x1, Pallas kernels, per_device(): pl.pallas_call(functools.partial(kernel, n_px, n_py), out_shape=(jax.Shap...  149 us

profile of v1, /device:TPU:25, one launch (start us, length us, event | category | flops | bytes accessed | tf_op | source)
XLA Modules:
  0.0 152.7 jit_solution(2221114773854357562)
XLA Ops:
  1.3 148.6 %cable_net.1 = (f32[3,1024,128]{2,1,0:T(8,128)}, f32[3,1024,128]{2,1,0:T(8,128)}, f32[16,64]{1,0:T(8,128)}, f32[16,64]{1,0:T(8,128)}, f32[1,128]{1,0:T(1,128)}) custom-call(f32[3,1024,128]{2,1,0:T(8,128)} %bitcast.4, f32[3,1024,128]{2,1,0:T(8,128)} %bitcast.5, f32[16,64]{1,0:T(8,128)} %anchor_h.1, f32[16,64]{1,0:T(8,128)} %q_down_h.1, f32[16,64]{1,0:T(8,128)} %q_right_h.1, ...), custom_call_target="tpu_custom_call" | custom-call | tf_op jit(solution)/shard_map/cable_net/pallas_call | solution.py:615
  149.8 2.8 %save.1 = (f32[3,1024,128]{2,1,0:T(8,128)}, f32[3,1024,128]{2,1,0:T(8,128)}, f32[16,64]{1,0:T(8,128)}, f32[16,64]{1,0:T(8,128)}, f32[1,128]{1,0:T(1,128)}) custom-call(f32[3,1024,128]{2,1,0:T(8,128)} %get-tuple-element.15.shape_in, f32[3,1024,128]{2,1,0:T(8,128)} %get-tuple-element.16.adjoint_in, f32[16,64]{1,0:T(8,128)} %get-tuple-element.17.down_in, ...), custom_call_target="tpu_custom_call" | custom-call | tf_op jit(solution)/shard_map/save/pallas_call | solution.py:705

commit v2 on v1

--- a/solution.py
+++ b/solution.py
@@ -73,11 +73,14 @@
 
 (
     S_P1, R_P1, S_P2, R_P2, S_UP, R_UP, S_DN, R_DN, S_LF, R_LF, S_RT, R_RT,
+    ONES,
+) = range(0, 78, 6)
+(
     S_CAB, R_CAB, S_DQ, R_DQ, S_QD, R_QD, S_QR, R_QR, S_SH, R_SH, S_AD, R_AD,
     S_GD, R_GD, S_GR, R_GR, S_HD, R_HD, S_HR, R_HR, L_B, L_T, L_S, L_A,
-    L_0, L_1, L_2, L_3, L_4, L_5, L_6, L_7,
-) = range(0, 88, 2)
-N_SEM = 88
+    L_0, L_1, L_2, L_3, L_4, L_5, L_6,
+) = range(ONES, ONES + 31)
+N_SEM = ONES + 31
 
 
 def kernel(
@@ -113,7 +116,7 @@
         for src, dst, s in (
             (cab_a_h, cab_a, L_0), (cab_b_h, cab_b, L_1),
             (cab_q_h, cab_q, L_3), (q_down_h, q_down, L_4), (q_right_h, q_right, L_5),
-            (rows_h, rows_v, L_6), (anchor_h, anchor, L_7),
+            (rows_h, rows_v, L_2), (anchor_h, anchor, L_6),
         )
     ]
     for copy in small:
@@ -241,11 +244,11 @@
     )
     L3[...] = jnp.concatenate([matrix, matrix - matrix.astype(BF16).astype(F32)], 1).astype(BF16)
 
-    def gather(src, dst):
+    def gather(src, dst, comps=(0, 1, 2)):
         def rows_of(w, carry):
             for e in range(8):
                 node = rows_s[0, (w + half * (e // 4)) * 4 + e % 4]
-                for c in range(3):
+                for c in comps:
                     dst[c, pl.ds(w * 8 + e, 1), :] = src[c, pl.ds(node, 1), :]
             return carry
 
@@ -259,16 +262,17 @@
 
     def send_all(src, dst, s, r):
         for h, q in peers:
-            remote(src.at[q], dst.at[py], s, r, (px, h * half + q)).start()
-        dst[py] = src[q0]
-
-    def send_lent():
+            remote(src.at[:, q], dst.at[:, py], s, r, (px, h * half + q)).start()
+        for c in range(3):
+            dst[c, py] = src[c, q0]
+
+    def send_lent(c):
         for h, q in near_peers:
-            remote(Y.at[q], recv1.at[q0], S_P1, R_P1, (px, h * half + q)).start()
-        recv1[q0] = Y[q0]
+            remote(Y.at[c, q], recv1.at[c, q0], S_P1 + c, R_P1 + c, (px, h * half + q)).start()
+        recv1[c, q0] = Y[c, q0]
 
     def put(dst, c, value):
-        dst[:, c] = value.reshape(dst.shape[0], 8, V)
+        dst[c] = value.reshape(dst.shape[1], 8, V)
 
     lax.fori_loop(0, half, gather_diag, 0)
     load_b.wait()
@@ -283,7 +287,7 @@
         d_l[c] = first
         x_l[c] = first
         put(Y, c, first)
-    send_lent()
+        send_lent(c)
     INV[...] = 1.0 / (GD[...] + dot(ONE[...], slot_sum))
 
     last = 2 * ROUNDS
@@ -294,39 +298,37 @@
     def spans(i):
         return pl.ds(pl.multiple_of(i * TY, TY), TY)
 
-    def scatter(lo, hi):
-        SF[lo * TY : hi * TY] = dot(ONE[lo * TY : hi * TY], F2[...])
-
-    def advance(i, a, b):
+    def lanes(c):
+        return slice(c * V, (c + 1) * V)
+
+    def scatter(c):
+        SF[TY : NODES - TY, lanes(c)] = dot(ONE[TY : NODES - TY], F2[:, lanes(c)])
+
+    def advance(c, i, a, b):
         at = spans(i)
-        inv = INV[at] * b
-        for c in range(3):
-            r = R[c, at] - SF[at, c * V : (c + 1) * V]
-            R[c, at] = r
-            d = a * D[c, at] + inv * r
-            D[c, at] = d
-            X[c, at] = X[c, at] + d
-
-    def begin(i):
+        r = R[c, at] - SF[at, lanes(c)]
+        R[c, at] = r
+        d = a * D[c, at] + (INV[at] * b) * r
+        D[c, at] = d
+        X[c, at] = X[c, at] + d
+
+    def begin(c, i):
         at = spans(i)
-        inv = INV[at] * (1.0 / THETA)
-        for c in range(3):
-            d = inv * R[c, at]
-            D[c, at] = d
-            X[c, at] = d
-
-    def turn(i, a, b):
+        d = INV[at] * (1.0 / THETA) * R[c, at]
+        D[c, at] = d
+        X[c, at] = d
+
+    def turn(c, i, a, b):
         at = spans(i)
         inv = INV[at]
-        for c in range(3):
-            r = R[c, at] - SF[at, c * V : (c + 1) * V]
-            x = X[c, at] + (a * D[c, at] + (inv * b) * r)
-            S[c, at] = x
-            r = x - T[c, at]
-            R[c, at] = r
-            d = inv * r * (1.0 / THETA)
-            D[c, at] = d
-            X[c, at] = d
+        r = R[c, at] - SF[at, lanes(c)]
+        x = X[c, at] + (a * D[c, at] + (inv * b) * r)
+        S[c, at] = x
+        r = x - T[c, at]
+        R[c, at] = r
+        d = inv * r * (1.0 / THETA)
+        D[c, at] = d
+        X[c, at] = d
 
     def each(fn, lo, hi):
         def body(i, carry):
@@ -335,16 +337,36 @@
 
         lax.fori_loop(lo, hi, body, 0)
 
-    def stencil(i, par, above, below):
+    def stencil(c, i, par, above, below):
         at = spans(i)
-        gd, wu, wd, wr, wl = GD[at], WD[at], WD[spans(i + 1)], WR[at], WL[at]
         row = iota((TY, V), 0)
-        for c in range(3):
-            d = D[c, at]
-            left = jnp.where(row == 0, lf[par, c, pl.ds(i, 1), :], pltpu.roll(d, 1, 0))
-            right = jnp.where(row == TY - 1, rt[par, c, pl.ds(i, 1), :], pltpu.roll(d, TY - 1, 0))
-            near = wu * above(c) + wd * below(c) + wl * left + wr * right
-            R[c, at] = R[c, at] - (gd * d - near)
+        d = D[c, at]
+        left = jnp.where(row == 0, lf[par, c, pl.ds(i, 1), :], pltpu.roll(d, 1, 0))
+        right = jnp.where(row == TY - 1, rt[par, c, pl.ds(i, 1), :], pltpu.roll(d, TY - 1, 0))
+        near = WD[at] * above + WD[spans(i + 1)] * below + WL[at] * left + WR[at] * right
+        R[c, at] = R[c, at] - (GD[at] * d - near)
+
+    def rims(c, par):
+        which = par * 3 + c
+        return (
+            remote(
+                D.at[c, pl.ds((TX - 1) * TY, TY)], up.at[par, c], S_UP + c, R_UP + which, (px_next, py)
+            ),
+            remote(D.at[c, pl.ds(0, TY)], dn.at[par, c], S_DN + c, R_DN + which, (px_prev, py)),
+        )
+
+    def sides(c, par):
+        which = par * 3 + c
+        return (
+            remote(cr.at[c], lf.at[par, c], S_LF + c, R_LF + which, (px, py_next)),
+            remote(cl.at[c], rt.at[par, c], S_RT + c, R_RT + which, (px, py_prev)),
+        )
+
+    for c in range(3):
+        begin(c, 0)
+        begin(c, TX - 1)
+        for copy in rims(c, 0):
+            copy.start()
 
     def stretches(view, store):
         at_a_, at_b_ = ends(cab_s[...], h0)
@@ -352,7 +374,7 @@
         total = None
         for c in range(3):
             out = None
-            for part in split3(view[:, c].reshape(128, V)):
+            for part in split3(view[c].reshape(128, V)):
                 piece = lax.dot_general(
                     inc_, part, (((0,), (0,)), ((), ())), preferred_element_type=F32
                 )
@@ -368,55 +390,48 @@
         par = t % 2
         first, middle = t == 0, t == ROUNDS
         usual = jnp.logical_and(t != 0, t != ROUNDS)
+        final, half_way = t == last - 1, t == ROUNDS - 1
         a_prev, b_prev = coef_of((t + ROUNDS - 1) % ROUNDS)
         a_next, b_next = coef_of(t % ROUNDS)
 
-        @pl.when(first)
-        def _():
-            begin(0)
-            begin(TX - 1)
-
-        @pl.when(usual)
-        def _():
-            advance(0, a_prev, b_prev)
-            advance(TX - 1, a_prev, b_prev)
-
-        @pl.when(middle)
-        def _():
-            turn(0, a_prev, b_prev)
-            turn(TX - 1, a_prev, b_prev)
-
-        to_next = remote(
-            D.at[:, pl.ds((TX - 1) * TY, TY)], up.at[par], S_UP, R_UP + par, (px_next, py)
-        )
-        to_prev = remote(D.at[:, pl.ds(0, TY)], dn.at[par], S_DN, R_DN + par, (px_prev, py))
-        to_next.start()
-        to_prev.start()
-
-        @pl.when(t != 0)
-        def _():
-            scatter(1, TX - 1)
-
-        @pl.when(first)
-        def _():
-            each(begin, 1, TX - 1)
-
-        @pl.when(usual)
-        def _():
-            each(lambda i: advance(i, a_prev, b_prev), 1, TX - 1)
-
-        @pl.when(middle)
-        def _():
-            each(lambda i: turn(i, a_prev, b_prev), 1, TX - 1)
-
-        for c in range(3):
+        for c in range(3):
+            @pl.when(first)
+            def _():
+                each(lambda i: begin(c, i), 1, TX - 1)
+
+            @pl.when(usual)
+            def _():
+                scatter(c)
+                each(lambda i: advance(c, i, a_prev, b_prev), 1, TX - 1)
+
+            @pl.when(middle)
+            def _():
+                scatter(c)
+                each(lambda i: turn(c, i, a_prev, b_prev), 1, TX - 1)
+
             for i in range(TX):
                 cl[c, i : i + 1] = D[c, i * TY : i * TY + 1]
                 cr[c, i : i + 1] = D[c, (i + 1) * TY - 1 : (i + 1) * TY]
-        to_right = remote(cr, lf.at[par], S_LF, R_LF + par, (px, py_next))
-        to_left = remote(cl, rt.at[par], S_RT, R_RT + par, (px, py_prev))
-        to_right.start()
-        to_left.start()
+            for copy in sides(c, par):
+                copy.start()
+
+        for c in range(3):
+            wait_bytes(recv1.at[c, pl.ds(0, half - 1)], R_P1 + c)
+            high, low = split2(recv1[c].reshape(SLOTS, V))
+            matrix = L3[...]
+            put(Fs, c, dot(matrix, jnp.concatenate([high, high], 0)) + dot(matrix[:, :SLOTS], low))
+            for h, q in peers:
+                to = h * half + q
+                remote(
+                    Fs.at[c, to], frecv.at[par, c, py], S_P2 + c, R_P2 + par * 3 + c, (px, to)
+                ).start()
+            frecv[par, c, py] = Fs[c, py]
+
+        @pl.when(first)
+        def _():
+            wait_bytes(dq_s.at[pl.ds(0, n_py - 1)], S_DQ)
+            load_t.wait()
+            gather(T, t_l)
 
         @pl.when(middle)
         def _():
@@ -427,91 +442,84 @@
             shape_down.start()
             shape_right.start()
 
-        wait_bytes(recv1.at[pl.ds(0, half - 1)], R_P1)
-        for c in range(3):
-            high, low = split2(recv1[:, c].reshape(SLOTS, V))
-            matrix = L3[...]
-            put(Fs, c, dot(matrix, jnp.concatenate([high, high], 0)) + dot(matrix[:, :SLOTS], low))
-        for h, q in peers:
-            to = h * half + q
-            remote(Fs.at[to], frecv.at[par, py], S_P2, R_P2 + par, (px, to)).start()
-        frecv[par, py] = Fs[py]
-
-        @pl.when(t == 0)
-        def _():
-            wait_bytes(dq_s.at[pl.ds(0, n_py - 1)], S_DQ)
-            load_t.wait()
-            gather(T, t_l)
-
         @pl.when(t == ROUNDS + 1)
         def _():
-            wait_bytes(recvS.at[pl.ds(0, n_py - 1)], R_SH)
-            wait_bytes(recvS.at[pl.ds(0, n_py - 1)], S_SH)
+            wait_bytes(recvS.at[:, pl.ds(0, n_py - 1)], R_SH)
+            wait_bytes(recvS.at[:, pl.ds(0, n_py - 1)], S_SH)
             stretches(recvS, True)
 
-        to_right.wait()
-        to_left.wait()
-        each(
-            lambda i: stencil(
-                i, par, lambda c: D[c, spans(i - 1)], lambda c: D[c, spans(i + 1)]
-            ),
-            1,
-            TX - 1,
-        )
-        to_next.wait()
-        to_prev.wait()
-        stencil(0, par, lambda c: up[par, c], lambda c: D[c, spans(1)])
-        stencil(TX - 1, par, lambda c: D[c, spans(TX - 2)], lambda c: dn[par, c])
-        gather(R, rg_l)
-        wait_bytes(recv1.at[pl.ds(0, half - 1)], S_P1)
-
-        wait_bytes(frecv.at[0, pl.ds(0, n_py - 1)], R_P2 + par)
-        for c in range(3):
-            high, low = split2((frecv[par, 0:half, c] + frecv[par, half:, c]).reshape(SLOTS, V))
-            lanes = pl.ds(c * V, V)
-            F2[0:SLOTS, lanes] = high
-            F2[SLOTS:, lanes] = low
-        at_node = dot(CR[...], F2[...])
-        for c in range(3):
-            r = rg_l[c] - at_node[:SLOTS, c * V : (c + 1) * V]
+        for c in range(3):
+            for copy in sides(c, par):
+                copy.wait()
+            each(
+                lambda i: stencil(c, i, par, D[c, spans(i - 1)], D[c, spans(i + 1)]), 1, TX - 1
+            )
+
+        for c in range(3):
+            for copy in rims(c, par):
+                copy.wait()
+            stencil(c, 0, par, up[par, c], D[c, spans(1)])
+            stencil(c, TX - 1, par, D[c, spans(TX - 2)], dn[par, c])
+            gather(R, rg_l, (c,))
+            wait_bytes(recv1.at[c, pl.ds(0, half - 1)], S_P1 + c)
+            wait_bytes(frecv.at[0, c, pl.ds(0, n_py - 1)], R_P2 + par * 3 + c)
+            high, low = split2((frecv[par, c, 0:half] + frecv[par, c, half:]).reshape(SLOTS, V))
+            F2[0:SLOTS, lanes(c)] = high
+            F2[SLOTS:, lanes(c)] = low
+            at_node = dot(CR[...], F2[:, lanes(c)])
+            r = rg_l[c] - at_node[:SLOTS]
             d = a_next * d_l[c] + (b_next * inv_l[...]) * r
+            x_l[c] = x_l[c] + d
             d_l[c] = d
-            x_l[c] = x_l[c] + d
-            put(Y, c, d)
-        SF[0:TY] = at_node[SLOTS : SLOTS + TY]
-        SF[NODES - TY :] = at_node[SLOTS + TY :]
-
-        @pl.when(t == ROUNDS - 1)
-        def _():
-            for c in range(3):
+
+            @pl.when(half_way)
+            def _():
                 put(XS, c, x_l[c])
-                d = inv_l[...] * (x_l[c] - t_l[c]) * (1.0 / THETA)
-                d_l[c] = d
-                x_l[c] = d
-                put(Y, c, d)
-
-        @pl.when(t != last - 1)
-        def _():
-            send_lent()
-
-        @pl.when(t == ROUNDS - 1)
+                d_l[c] = inv_l[...] * (x_l[c] - t_l[c]) * (1.0 / THETA)
+                x_l[c] = d_l[c]
+
+            @pl.when(jnp.logical_not(final))
+            def _():
+                put(Y, c, d_l[c])
+                send_lent(c)
+
+            SF[0:TY, lanes(c)] = at_node[SLOTS : SLOTS + TY]
+            SF[NODES - TY :, lanes(c)] = at_node[SLOTS + TY :]
+
+            @pl.when(half_way)
+            def _():
+                turn(c, 0, a_next, b_next)
+                turn(c, TX - 1, a_next, b_next)
+
+            @pl.when(jnp.logical_not(half_way))
+            def _():
+                advance(c, 0, a_next, b_next)
+                advance(c, TX - 1, a_next, b_next)
+
+            @pl.when(jnp.logical_not(final))
+            def _():
+                for copy in rims(c, 1 - par):
+                    copy.start()
+
+        @pl.when(half_way)
         def _():
             send_all(XS, recvS, S_SH, R_SH)
 
-        wait_bytes(frecv.at[0, pl.ds(0, n_py - 1)], S_P2)
+        for c in range(3):
+            wait_bytes(frecv.at[0, c, pl.ds(0, n_py - 1)], S_P2 + c)
         return carry
 
     lax.fori_loop(0, last, round_, 0)
 
+    adjoint_down = remote(X.at[:, pl.ds(0, TY)], gdA, S_HD, R_HD, (px_prev, py))
+    adjoint_down.start()
     for c in range(3):
         put(Y, c, x_l[c])
     send_all(Y, recvA, S_AD, R_AD)
     a, b = COEF[-1]
-    advance(0, a, b)
-    adjoint_down = remote(X.at[:, pl.ds(0, TY)], gdA, S_HD, R_HD, (px_prev, py))
-    adjoint_down.start()
-    scatter(1, TX - 1)
-    each(lambda i: advance(i, a, b), 1, TX)
+    for c in range(3):
+        scatter(c)
+        each(lambda i: advance(c, i, a, b), 1, TX - 1)
     save_adjoint = pltpu.make_async_copy(X, adjoint_out, sem.at[L_A])
     save_adjoint.start()
     for c in range(3):
@@ -569,10 +577,10 @@
     down_out[...] = jnp.where(gi < n_px * TX - 1, down_out[...], 0.0)
     right_out[...] = jnp.where(gj < n_py * TY - 1, right_out[...], 0.0)
 
-    wait_bytes(recvA.at[pl.ds(0, n_py - 1)], R_AD)
+    wait_bytes(recvA.at[:, pl.ds(0, n_py - 1)], R_AD)
     long_sums = lane_sums(stretches(recvA, False))
     long_out[...] = jnp.where(live, long_sums, 0.0)
-    wait_bytes(recvA.at[pl.ds(0, n_py - 1)], S_AD)
+    wait_bytes(recvA.at[:, pl.ds(0, n_py - 1)], S_AD)
     save_shape.wait()
     save_adjoint.wait()
 
@@ -611,7 +619,7 @@
     def scratch(*shape, dtype=F32):
         return pltpu.VMEM(shape, dtype)
 
-    lent = (half, 3, 8, V)
+    lent = (3, half, 8, V)
     results = pl.pallas_call(
         functools.partial(kernel, n_px, n_py),
         out_shape=(
@@ -649,10 +657,10 @@
             scratch(*lent),
             scratch(*lent),
             scratch(*lent),
-            scratch(n_py, 3, 8, V),
-            scratch(n_py, 3, 8, V),
-            scratch(n_py, 3, 8, V),
-            scratch(2, n_py, 3, 8, V),
+            scratch(3, n_py, 8, V),
+            scratch(3, n_py, 8, V),
+            scratch(3, n_py, 8, V),
+            scratch(2, 3, n_py, 8, V),
             scratch(2, 3, TY, V),
             scratch(2, 3, TY, V),
             scratch(2, 3, TX, V),

time: 153 us -> 147 us (0.961)
  Pallas kernels: 151 us -> 146 us
    pallas_call x1, Pallas kernels: 149 us -> 143 us  [per_device(): pl.pallas_call(functools.partial(kernel, n_px, n_py), out_shape=(jax.Shap...]
where the time goes in v2:
time: 147 us
  Pallas kernels  146 us (99%)
    pallas_call x1, Pallas kernels, per_device(): pl.pallas_call(functools.partial(kernel, n_px, n_py), out_shape=(jax.Shap...  143 us

profile of v2, /device:TPU:25, one launch (start us, length us, event | category | flops | bytes accessed | tf_op | source)
XLA Modules:
  0.0 147.0 jit_solution(601237618647312316)
XLA Ops:
  1.3 142.9 %cable_net.1 = (f32[3,1024,128]{2,1,0:T(8,128)}, f32[3,1024,128]{2,1,0:T(8,128)}, f32[16,64]{1,0:T(8,128)}, f32[16,64]{1,0:T(8,128)}, f32[1,128]{1,0:T(1,128)}) custom-call(f32[3,1024,128]{2,1,0:T(8,128)} %bitcast.4, f32[3,1024,128]{2,1,0:T(8,128)} %bitcast.5, f32[16,64]{1,0:T(8,128)} %anchor_h.1, f32[16,64]{1,0:T(8,128)} %q_down_h.1, f32[16,64]{1,0:T(8,128)} %q_right_h.1, ...), custom_call_target="tpu_custom_call" | custom-call | tf_op jit(solution)/shard_map/cable_net/pallas_call | solution.py:623
  144.1 2.8 %save.1 = (f32[3,1024,128]{2,1,0:T(8,128)}, f32[3,1024,128]{2,1,0:T(8,128)}, f32[16,64]{1,0:T(8,128)}, f32[16,64]{1,0:T(8,128)}, f32[1,128]{1,0:T(1,128)}) custom-call(f32[3,1024,128]{2,1,0:T(8,128)} %get-tuple-element.15.shape_in, f32[3,1024,128]{2,1,0:T(8,128)} %get-tuple-element.16.adjoint_in, f32[16,64]{1,0:T(8,128)} %get-tuple-element.17.down_in, ...), custom_call_target="tpu_custom_call" | custom-call | tf_op jit(solution)/shard_map/save/pallas_call | solution.py:713

commit v3 on v2

--- a/solution.py
+++ b/solution.py
@@ -355,6 +355,9 @@
             remote(D.at[c, pl.ds(0, TY)], dn.at[par, c], S_DN + c, R_DN + which, (px_prev, py)),
         )
 
+    def early(c):
+        return (2, 1, 1)[c]
+
     def sides(c, par):
         which = par * 3 + c
         return (
@@ -365,7 +368,7 @@
     for c in range(3):
         begin(c, 0)
         begin(c, TX - 1)
-        for copy in rims(c, 0):
+        for copy in rims(c, 0)[: early(c)]:
             copy.start()
 
     def stretches(view, store):
@@ -426,6 +429,8 @@
                     Fs.at[c, to], frecv.at[par, c, py], S_P2 + c, R_P2 + par * 3 + c, (px, to)
                 ).start()
             frecv[par, c, py] = Fs[c, py]
+            for copy in rims(c, par)[early(c) :]:
+                copy.start()
 
         @pl.when(first)
         def _():
@@ -498,7 +503,7 @@
 
             @pl.when(jnp.logical_not(final))
             def _():
-                for copy in rims(c, 1 - par):
+                for copy in rims(c, 1 - par)[: early(c)]:
                     copy.start()
 
         @pl.when(half_way)

time: 147 us -> 134 us (0.912)
  Pallas kernels: 146 us -> 133 us
    pallas_call x1, Pallas kernels: 143 us -> 130 us  [per_device(): pl.pallas_call(functools.partial(kernel, n_px, n_py), out_shape=(jax.Shap...]
where the time goes in v3:
time: 134 us
  Pallas kernels  133 us (99%)
    pallas_call x1, Pallas kernels, per_device(): pl.pallas_call(functools.partial(kernel, n_px, n_py), out_shape=(jax.Shap...  130 us
    pallas_call x1, Pallas kernels, per_device(): pl.pallas_call(save_kernel, out_shape=[jax.ShapeDtypeStruct(r.shape, F32)...  2.85 us

profile of v3, /device:TPU:25, one launch (start us, length us, event | category | flops | bytes accessed | tf_op | source)
XLA Modules:
  0.0 134.1 jit_solution(16803004763443865775)
XLA Ops:
  1.3 130.0 %cable_net.1 = (f32[3,1024,128]{2,1,0:T(8,128)}, f32[3,1024,128]{2,1,0:T(8,128)}, f32[16,64]{1,0:T(8,128)}, f32[16,64]{1,0:T(8,128)}, f32[1,128]{1,0:T(1,128)}) custom-call(f32[3,1024,128]{2,1,0:T(8,128)} %bitcast.4, f32[3,1024,128]{2,1,0:T(8,128)} %bitcast.5, f32[16,64]{1,0:T(8,128)} %anchor_h.1, f32[16,64]{1,0:T(8,128)} %q_down_h.1, f32[16,64]{1,0:T(8,128)} %q_right_h.1, ...), custom_call_target="tpu_custom_call" | custom-call | tf_op jit(solution)/shard_map/cable_net/pallas_call | solution.py:628
  131.3 2.8 %save.1 = (f32[3,1024,128]{2,1,0:T(8,128)}, f32[3,1024,128]{2,1,0:T(8,128)}, f32[16,64]{1,0:T(8,128)}, f32[16,64]{1,0:T(8,128)}, f32[1,128]{1,0:T(1,128)}) custom-call(f32[3,1024,128]{2,1,0:T(8,128)} %get-tuple-element.15.shape_in, f32[3,1024,128]{2,1,0:T(8,128)} %get-tuple-element.16.adjoint_in, f32[16,64]{1,0:T(8,128)} %get-tuple-element.17.down_in, ...), custom_call_target="tpu_custom_call" | custom-call | tf_op jit(solution)/shard_map/save/pallas_call | solution.py:718

commit v4 on v3

--- a/solution.py
+++ b/solution.py
@@ -266,6 +266,11 @@
         for c in range(3):
             dst[c, py] = src[c, q0]
 
+    def send_comp(src, dst, c, s, r):
+        for h, q in peers:
+            remote(src.at[c, q], dst.at[c, py], s, r, (px, h * half + q)).start()
+        dst[c, py] = src[c, q0]
+
     def send_lent(c):
         for h, q in near_peers:
             remote(Y.at[c, q], recv1.at[c, q0], S_P1 + c, R_P1 + c, (px, h * half + q)).start()
@@ -288,7 +293,9 @@
         x_l[c] = first
         put(Y, c, first)
         send_lent(c)
-    INV[...] = 1.0 / (GD[...] + dot(ONE[...], slot_sum))
+    on_rims = dot(CR[SLOTS:], slot_sum)
+    INV[0:TY] = 1.0 / (GD[0:TY] + on_rims[:TY])
+    INV[NODES - TY :] = 1.0 / (GD[NODES - TY :] + on_rims[TY:])
 
     last = 2 * ROUNDS
     save_shape = pltpu.make_async_copy(S, shape_out, sem.at[L_S])
@@ -370,6 +377,8 @@
         begin(c, TX - 1)
         for copy in rims(c, 0)[: early(c)]:
             copy.start()
+    inner = slice(TY, NODES - TY)
+    INV[inner] = 1.0 / (GD[inner] + dot(ONE[inner], slot_sum))
 
     def stretches(view, store):
         at_a_, at_b_ = ends(cab_s[...], h0)
@@ -444,10 +453,14 @@
                 for i in range(TX):
                     c0S[c, i : i + 1] = S[c, i * TY : i * TY + 1]
             save_shape.start()
+            send_all(XS, recvS, S_SH, R_SH)
+
+        @pl.when(t == ROUNDS + 1)
+        def _():
             shape_down.start()
             shape_right.start()
 
-        @pl.when(t == ROUNDS + 1)
+        @pl.when(t == ROUNDS + 3)
         def _():
             wait_bytes(recvS.at[:, pl.ds(0, n_py - 1)], R_SH)
             wait_bytes(recvS.at[:, pl.ds(0, n_py - 1)], S_SH)
@@ -506,9 +519,11 @@
                 for copy in rims(c, 1 - par)[: early(c)]:
                     copy.start()
 
-        @pl.when(half_way)
-        def _():
-            send_all(XS, recvS, S_SH, R_SH)
+            @pl.when(final)
+            def _():
+                put(Y, c, x_l[c])
+                send_comp(Y, recvA, c, S_AD, R_AD)
+                remote(X.at[c, pl.ds(0, TY)], gdA.at[c], S_HD, R_HD, (px_prev, py)).start()
 
         for c in range(3):
             wait_bytes(frecv.at[0, c, pl.ds(0, n_py - 1)], S_P2 + c)
@@ -517,10 +532,6 @@
     lax.fori_loop(0, last, round_, 0)
 
     adjoint_down = remote(X.at[:, pl.ds(0, TY)], gdA, S_HD, R_HD, (px_prev, py))
-    adjoint_down.start()
-    for c in range(3):
-        put(Y, c, x_l[c])
-    send_all(Y, recvA, S_AD, R_AD)
     a, b = COEF[-1]
     for c in range(3):
         scatter(c)

time: 134 us -> 132 us (0.985)
  Pallas kernels: 133 us -> 130 us
    pallas_call x1, Pallas kernels: 130 us -> 127 us  [per_device(): pl.pallas_call(functools.partial(kernel, n_px, n_py), out_shape=(jax.Shap...]
where the time goes in v4:
time: 132 us; the launch traced here: 131 us
  Pallas kernels  130 us (98%)
    pallas_call x1, Pallas kernels, per_device(): pl.pallas_call(functools.partial(kernel, n_px, n_py), out_shape=(jax.Shap...  127 us
    pallas_call x1, Pallas kernels, per_device(): pl.pallas_call(save_kernel, out_shape=[jax.ShapeDtypeStruct(r.shape, F32)...  2.85 us

profile of v4, /device:TPU:25, one launch (start us, length us, event | category | flops | bytes accessed | tf_op | source)
XLA Modules:
  0.0 131.1 jit_solution(11435296637802641837)
XLA Ops:
  1.3 127.0 %cable_net.1 = (f32[3,1024,128]{2,1,0:T(8,128)}, f32[3,1024,128]{2,1,0:T(8,128)}, f32[16,64]{1,0:T(8,128)}, f32[16,64]{1,0:T(8,128)}, f32[1,128]{1,0:T(1,128)}) custom-call(f32[3,1024,128]{2,1,0:T(8,128)} %bitcast.4, f32[3,1024,128]{2,1,0:T(8,128)} %bitcast.5, f32[16,64]{1,0:T(8,128)} %anchor_h.1, f32[16,64]{1,0:T(8,128)} %q_down_h.1, f32[16,64]{1,0:T(8,128)} %q_right_h.1, ...), custom_call_target="tpu_custom_call" | custom-call | tf_op jit(solution)/shard_map/cable_net/pallas_call | solution.py:639
  128.3 2.8 %save.1 = (f32[3,1024,128]{2,1,0:T(8,128)}, f32[3,1024,128]{2,1,0:T(8,128)}, f32[16,64]{1,0:T(8,128)}, f32[16,64]{1,0:T(8,128)}, f32[1,128]{1,0:T(1,128)}) custom-call(f32[3,1024,128]{2,1,0:T(8,128)} %get-tuple-element.15.shape_in, f32[3,1024,128]{2,1,0:T(8,128)} %get-tuple-element.16.adjoint_in, f32[16,64]{1,0:T(8,128)} %get-tuple-element.17.down_in, ...), custom_call_target="tpu_custom_call" | custom-call | tf_op jit(solution)/shard_map/save/pallas_call | solution.py:729

commit v5 on v4

--- a/solution.py
+++ b/solution.py
@@ -89,7 +89,7 @@
     shape_out, adjoint_out, down_out, right_out, long_out,
     R, D, X, S, T, SF, GD, WD, WR, WL, INV, ONE, F2, CR, L3, IO, IP,
     rg_l, d_l, x_l, t_l, inv_l, Y, XS, recv1, recvS, recvA, Fs, frecv,
-    up, dn, lf, rt, cl, cr, cab_s, cab_r, dq_s, dq_r, qd_s, qd_r, qr_s, qr_r,
+    ud, lf, rt, cl, cr, cab_s, cab_r, dq_s, dq_r, qd_s, qd_r, qr_s, qr_r,
     gdS, grS, gdA, grA, c0S, c0A, stS, PD, PR,
     anchor, q_down, q_right, rows_v, cab_a, cab_b, cab_q, sem,
 ):
@@ -354,13 +354,16 @@
         R[c, at] = R[c, at] - (GD[at] * d - near)
 
     def rims(c, par):
-        which = par * 3 + c
-        return (
-            remote(
-                D.at[c, pl.ds((TX - 1) * TY, TY)], up.at[par, c], S_UP + c, R_UP + which, (px_next, py)
-            ),
-            remote(D.at[c, pl.ds(0, TY)], dn.at[par, c], S_DN + c, R_DN + which, (px_prev, py)),
-        )
+        def one(s, is_next):
+            row = pl.multiple_of(is_next * ((TX - 1) * TY), TY)
+            to = (px + n_px - 1 + 2 * is_next) % n_px
+            r = R_UP + (1 - is_next) * (R_DN - R_UP) + par * 3 + c
+            return remote(
+                D.at[c, pl.ds(row, TY)], ud.at[par, c, 1 - is_next], s + c, r, (to, py)
+            )
+
+        odd = px % 2
+        return one(S_UP, odd), one(S_DN, 1 - odd)
 
     def early(c):
         return (2, 1, 1)[c]
@@ -476,8 +479,8 @@
         for c in range(3):
             for copy in rims(c, par):
                 copy.wait()
-            stencil(c, 0, par, up[par, c], D[c, spans(1)])
-            stencil(c, TX - 1, par, D[c, spans(TX - 2)], dn[par, c])
+            stencil(c, 0, par, ud[par, c, 0], D[c, spans(1)])
+            stencil(c, TX - 1, par, D[c, spans(TX - 2)], ud[par, c, 1])
             gather(R, rg_l, (c,))
             wait_bytes(recv1.at[c, pl.ds(0, half - 1)], S_P1 + c)
             wait_bytes(frecv.at[0, c, pl.ds(0, n_py - 1)], R_P2 + par * 3 + c)
@@ -677,8 +680,7 @@
             scratch(3, n_py, 8, V),
             scratch(3, n_py, 8, V),
             scratch(2, 3, n_py, 8, V),
-            scratch(2, 3, TY, V),
-            scratch(2, 3, TY, V),
+            scratch(2, 3, 2, TY, V),
             scratch(2, 3, TX, V),
             scratch(2, 3, TX, V),
             scratch(3, TX, V),

time: 132 us -> 132 us (level)
  no operation moved by 1% of the time
where the time goes in v5:
time: 132 us; the launch traced here: 131 us
  Pallas kernels  130 us (98%)
    pallas_call x1, Pallas kernels, per_device(): pl.pallas_call(functools.partial(kernel, n_px, n_py), out_shape=(jax.Shap...  127 us
    pallas_call x1, Pallas kernels, per_device(): pl.pallas_call(save_kernel, out_shape=[jax.ShapeDtypeStruct(r.shape, F32)...  2.85 us

profile of v5, /device:TPU:25, one launch (start us, length us, event | category | flops | bytes accessed | tf_op | source)
XLA Modules:
  0.0 131.2 jit_solution(1785682913859663030)
XLA Ops:
  1.3 127.1 %cable_net.1 = (f32[3,1024,128]{2,1,0:T(8,128)}, f32[3,1024,128]{2,1,0:T(8,128)}, f32[16,64]{1,0:T(8,128)}, f32[16,64]{1,0:T(8,128)}, f32[1,128]{1,0:T(1,128)}) custom-call(f32[3,1024,128]{2,1,0:T(8,128)} %bitcast.4, f32[3,1024,128]{2,1,0:T(8,128)} %bitcast.5, f32[16,64]{1,0:T(8,128)} %anchor_h.1, f32[16,64]{1,0:T(8,128)} %q_down_h.1, f32[16,64]{1,0:T(8,128)} %q_right_h.1, ...), custom_call_target="tpu_custom_call" | custom-call | tf_op jit(solution)/shard_map/cable_net/pallas_call | solution.py:642
  128.4 2.8 %save.1 = (f32[3,1024,128]{2,1,0:T(8,128)}, f32[3,1024,128]{2,1,0:T(8,128)}, f32[16,64]{1,0:T(8,128)}, f32[16,64]{1,0:T(8,128)}, f32[1,128]{1,0:T(1,128)}) custom-call(f32[3,1024,128]{2,1,0:T(8,128)} %get-tuple-element.15.shape_in, f32[3,1024,128]{2,1,0:T(8,128)} %get-tuple-element.16.adjoint_in, f32[16,64]{1,0:T(8,128)} %get-tuple-element.17.down_in, ...), custom_call_target="tpu_custom_call" | custom-call | tf_op jit(solution)/shard_map/save/pallas_call | solution.py:731
